TPU v7x, 32 devices: a whole 2x2x4 slice. The times are simulated.
32 devices in a mesh: gx: 4 (over y, x), gy: 2 (over core), gz: 4 (over z).
Axes of the slice: x: 2, y: 2, z: 4, core: 2. Of those that a mesh axis runs over, the one named last changes fastest.
Arguments:
- state: float32 [7, 4, 2, 32768], P(None, 'gx', 'gy', 'gz'), as said below
- tile_lists: int32 [4, 2, 256, 8], P('gx', 'gy', 'gz'), may hold values from 0 to 63
- tile_counts: int32 [4, 2, 256], P('gx', 'gy', 'gz'), may hold values from 1 to 8, as said below
- ghost_counts: int32 [4, 2, 4, 4], P('gx', 'gy', 'gz'), may hold values from 1 to 12
- cell_index: int32 [4, 2, 32768], P('gx', 'gy', 'gz'), may hold values from 0 to 4095, as said below
- fluid_vel: float32 [3, 4, 2, 4096], P(None, 'gx', 'gy', 'gz'), may hold values from -6 to 6
- fluid_frac: float32 [4, 2, 4096], P('gx', 'gy', 'gz'), may hold values from 0.4 to 0.9
Outputs:
- velocity_new: float32 [3, 4, 2, 32768], P(None, 'gx', 'gy', 'gz')
- fluid_new: float32 [3, 4, 2, 4096], P(None, 'gx', 'gy', 'gz')
Inputs may be any that keep to these rules, and one draw needn't show every extreme that they name: `state`: rows 0 to 2 are positions within 0 to 1, rows 3 to 5 velocities, row 6 radii within 0.15 to 0.35. `tile_counts`: in every box the first tile's count is the largest of that box. `cell_index`: A particle of box z along z has its cell in that box's slab, cells z * 1024 to (z + 1) * 1024 - 1, or in the slab of a box beside it along z.
All inputs are finite; a program needn't handle non-finite values.
Results may differ from a plain program's by a relative error of at most 0.0003.
Values sent between devices are 32-bit elements; how exact they have to be, the bound alone decides.
No kernel may reach another device: no remote copies, remote signals or barrier semaphores. Data moves between devices by JAX's collectives and lax.ppermute only.
A program may use at most 64 MiB of HBM per device.

v0:
```python
import functools

import jax
import jax.numpy as jnp
from jax import lax
from jax.experimental import pallas as pl
from jax.experimental.pallas import tpu as pltpu
from jax.sharding import PartitionSpec as P

TILE = 128
K = 8
NT = 64
GB = 12
FACE = 16
LANES = 128

stiffness = 5.0
damping = 2.0
time_step = 0.25
drag_coef = 64.0
fluid_density = 2.0
radius_ref = 0.25
spring = stiffness / damping

f32 = jnp.float32
bf16 = jnp.bfloat16

NROW = 32
VROW = 16
DUMMY = NT
GHOST = NT + 4
NFAR = GHOST + 4 * FACE
SIZES = (64, 32, 16)
GROUP = 16
EARLY = 2
KEPT = 64
SLOTS = NT * 6


def parts_of(q):
    first = q.astype(bf16).astype(f32)
    rest = q - first
    second = rest.astype(bf16).astype(f32)
    return first, second, (rest - second).astype(bf16).astype(f32)


ORDER = ((0, 0), (0, 1), (0, 2), (1, 0), (1, 1), (2, 0))


def centred(position):
    return position - 0.5


def geometry(columns):
    x, y, z = (centred(columns[k]) for k in range(3))
    r = columns[6]
    return (x, y, z, r), r * r - (x * x + y * y + z * z)


def near_rows(columns):
    lengths, own = geometry(columns)
    one = jnp.ones_like(own)
    rows = []
    for q in lengths:
        cut = parts_of(q)
        rows += [2.0 * cut[j] for _, j in ORDER]
    return rows + [one] * 3 + list(parts_of(own))


def far_rows(columns):
    lengths, own = geometry(columns)
    one = jnp.ones_like(own)
    rows = []
    for q in lengths:
        cut = parts_of(q)
        rows += [cut[i] for i, _ in ORDER]
    return rows + list(parts_of(own)) + [one] * 3


def value_rows(columns, living):
    cuts = [parts_of((columns[3 + c] - spring * centred(columns[c]))) for c in range(3)]
    return [cuts[c][k] * living for k in range(3) for c in range(3)] + [living]


def load(pairs, sems):
    copies = [pltpu.make_async_copy(source, target, sems.at[k]) for k, (source, target) in enumerate(pairs)]
    for copy in copies:
        copy.start()
    return copies


def pair_sums(far, near, values):
    weight = jnp.concatenate(
        [jnp.dot(left, right, preferred_element_type=f32) for left, right in zip(far, near)], axis=0
    )
    weight = jnp.maximum(weight, 0.0)
    coarse = weight.astype(bf16)
    fine = (weight - coarse.astype(f32)).astype(bf16)
    both = jnp.dot(values, jnp.concatenate([coarse, fine], axis=1), preferred_element_type=f32)
    return both[:, :TILE] + both[:, TILE:]


def interior_steps(begin, steps, size, carry, work_ref, near_ref, turned_ref, value_ref, acc_ref):
    def near_block(t, s):
        start = t * 128 + 96 - NROW * jnp.bitwise_and(s, 3)
        return near_ref[pl.ds(pl.multiple_of(start, NROW), 128), :]

    def far_block(s):
        return turned_ref[pl.ds(pl.multiple_of(lax.shift_right_logical(s, 2) * 128, 128), 128), :]

    def value_block(s):
        return value_ref[pl.ds(pl.multiple_of(s * VROW, VROW), VROW), :]

    def step(group, carry):
        sums = []
        for d in range(size):
            word = work_ref[begin + group * size + d]
            t = lax.shift_right_logical(word, 16)
            a = jnp.bitwise_and(lax.shift_right_logical(word, 8), 255)
            b = jnp.bitwise_and(word, 255)
            near = jnp.minimum(t, NT - 1)
            total = pair_sums(
                (far_block(a), far_block(b)),
                (near_block(near, a), near_block(near, b)),
                jnp.concatenate([value_block(a), value_block(b)], axis=1),
            )
            sums.append((t, total))
        last, running = carry
        for t, total in sums:
            running = total + jnp.where(t == last, running, 0.0)
            acc_ref[pl.ds(pl.multiple_of(t * VROW, VROW), VROW), :] = running
            last = t
        return last, running

    return lax.fori_loop(0, steps, step, carry)


def deposit_kernel(
    state_hbm, cell_hbm, vel_hbm, frac_hbm, ghost_hbm,
    parts_ref, xa_ref, xb_ref, ya_ref, yb_ref, state_ref, cell_ref,
    vel_ref, frac_ref, source_ref, deposit_ref, total_ref, ghost_ref, sems,
):
    copies = load(
        [
            (state_hbm, state_ref), (cell_hbm, cell_ref), (vel_hbm, vel_ref), (frac_hbm, frac_ref),
            (ghost_hbm, ghost_ref),
        ],
        sems,
    )
    slab = vel_ref.shape[1]
    wide = 3 * slab
    bands = wide // 2
    even_x, even_y = (jnp.bitwise_and(lax.axis_index(axis), 1) == 0 for axis in ("gx", "gy"))
    first_band = (lax.axis_index("gz") - 1) * (slab // 2)
    for copy in copies:
        copy.wait()

    r = state_ref[6]
    rate = drag_coef * r * r
    sources = [rate * state_ref[3 + c] for c in range(3)] + [rate]
    for c, source in enumerate(sources):
        for k, part in enumerate(parts_of(source)[:2]):
            source_ref[pl.ds(4 * k + c, NT, stride=8), :] = part
    low_of = lax.broadcasted_iota(jnp.int32, (2 * LANES, LANES), 0)

    def add_group(group, total):
        cells = cell_ref[pl.ds(pl.multiple_of(group * 8, 8), 8), :]
        band = lax.shift_right_logical(cells, 8) - first_band
        low = jnp.bitwise_and(cells, 255)
        left, right = [], []
        for t in range(8):
            rows = source_ref[pl.ds(pl.multiple_of(group * 64 + t * 8, 8), 8), :]
            here = jnp.broadcast_to(band[t : t + 1, :], (8, LANES))
            left.append(jnp.concatenate([jnp.where(here == h, rows, 0.0) for h in range(bands)], axis=0).astype(bf16))
            right.append(jnp.where(low[t : t + 1, :] == low_of, 1.0, 0.0).astype(bf16))
        added = lax.dot_general(
            jnp.concatenate(left, axis=1),
            jnp.concatenate(right, axis=1),
            (((1,), (1,)), ((), ())),
            preferred_element_type=f32,
        )
        deposit_ref[0] += added[:, :LANES]
        deposit_ref[1] += added[:, LANES:]
        return total

    deposit_ref[...] = jnp.zeros_like(deposit_ref)
    lax.fori_loop(0, NT // 8, add_group, 0, unroll=8)
    frac = fluid_density * frac_ref[...]
    for c in range(4):
        for k in range(2):
            both = deposit_ref[k, pl.ds(c, bands, stride=8), :] + deposit_ref[k, pl.ds(4 + c, bands, stride=8), :]
            total_ref[pl.ds(k, bands, stride=2), :] = both * time_step
        below, here, above = (total_ref[pl.ds(k * slab, slab), :] for k in range(3))
        parts_ref[c] = above
        parts_ref[4 + c] = here + (frac * vel_ref[c] if c < 3 else frac)
        parts_ref[8 + c] = below
    order = lax.broadcasted_iota(jnp.int32, (FACE, TILE), 0)
    for low, even, a_ref, b_ref in ((0, even_x, xa_ref, xb_ref), (2, even_y, ya_ref, yb_ref)):
        for k in range(7):
            lower = state_ref[k, low * GB : (low + 1) * GB, :]
            upper = state_ref[k, (low + 1) * GB : (low + 2) * GB, :]
            a_ref[k, 0:GB, :] = jnp.where(even, upper, lower)
            b_ref[k, 0:GB, :] = jnp.where(even, lower, upper)
            a_ref[k, GB:FACE, :] = jnp.zeros((FACE - GB, TILE), f32)
            b_ref[k, GB:FACE, :] = jnp.zeros((FACE - GB, TILE), f32)
        lower, upper = ghost_ref[low], ghost_ref[low + 1]
        a_ref[7] = jnp.where(order < jnp.where(even, upper, lower), 1.0, 0.0)
        b_ref[7] = jnp.where(order < jnp.where(even, lower, upper), 1.0, 0.0)

def inner_outer():
    z = lax.axis_index("gz")
    lower = z < 2
    return lower, jnp.bitwise_and(z, 1) == jnp.where(lower, 1, 0)


def put_rows(ref, first, rows, stride, filled):
    tiles = rows[0].shape[0]
    all_rows = jnp.stack(rows + [jnp.zeros_like(rows[0])] * (filled - len(rows)), axis=0)
    ref[first * stride : (first + tiles) * stride, :] = jnp.swapaxes(all_rows, 0, 1).reshape(tiles * stride, TILE)


def facing(flag, ref):
    return [jnp.where(flag, ref[c], ref[8 + c]) for c in range(4)]


def ghost_slots():
    slot_of, beside = [], []
    for axis in ("gx", "gy"):
        place, count = lax.axis_index(axis), lax.axis_size(axis)
        first = max(slot_of, default=-1) + 1
        slot_of += [first, first if count == 2 else first + 1]
        beside += [place > 0, place < count - 1]
    return slot_of, beside


def feature_kernel(paired, lists_hbm, counts_hbm, ghost_hbm, state_ref, *refs):
    if paired:
        parts_ref, beside_ref, *refs = refs
    near16_ref, turned_ref, value16_ref, acc_ref, work_ref, *refs = refs
    if paired:
        across_ref, *refs = refs
    near_ref, far_ref, value_ref, lists_ref, counts_ref, ghost_ref, sems = refs
    copies = load([(lists_hbm, lists_ref), (counts_hbm, counts_ref), (ghost_hbm, ghost_ref)], sems)
    if paired:
        lower, inner = inner_outer()
        mine, other = facing(lower, parts_ref), facing(lower, beside_ref)
        for c in range(4):
            across_ref[c] = jnp.where(inner, parts_ref[4 + c] + other[c], beside_ref[4 + c] + mine[c])
            across_ref[4 + c] = jnp.where(inner, mine[c], other[c])
    near16_ref[pl.ds(NT * 128, 128), :] = jnp.zeros((128, TILE), bf16)
    turned_ref[DUMMY * NROW : GHOST * NROW, :] = jnp.zeros((4 * NROW, TILE), bf16)
    value16_ref[DUMMY * VROW : GHOST * VROW, :] = jnp.zeros((4 * VROW, TILE), bf16)

    columns = [state_ref[k] for k in range(7)]
    put_rows(near_ref, 0, near_rows(columns), NROW, NROW)
    put_rows(far_ref, 0, far_rows(columns), NROW, NROW)
    put_rows(value_ref, 0, value_rows(columns, jnp.ones((NT, TILE), f32)), VROW, VROW)
    slot_of, beside = ghost_slots()
    for copy in copies:
        copy.wait()
    alive = [jnp.where(beside[face], ghost_ref[face], 0) for face in range(4)]
    n = jnp.int32(0)
    for b in [*range(4 * GB // 4, NT // 4), *range(4 * GB // 4)]:
        if b == 0:
            without_ghosts = n
        rows = slice(b * 128, (b + 1) * 128)
        turned_ref[rows, :] = far_ref[rows, :].T.astype(bf16)
        rows = slice(b * 4 * VROW, (b + 1) * 4 * VROW)
        value16_ref[rows, :] = value_ref[rows, :].astype(bf16)
        for t in range(4 * b, 4 * b + 4):
            near16_ref[t * 128 : (t + 1) * 128, :] = jnp.concatenate(
                [jnp.zeros((96, TILE), bf16), near_ref[t * NROW : (t + 1) * NROW, :].astype(bf16)], axis=0
            )
            count = counts_ref[t]
            face, place = t // GB, t % GB
            if face < 4:
                ghost = GHOST + slot_of[face] * FACE + place
                entries = count + (place < alive[face]).astype(jnp.int32)
            else:
                ghost, entries = DUMMY, count
            for d in range((K + 1 + (face < 4)) // 2):
                a = lists_ref[min(2 * d, K - 1), t]
                if face < 4 and d > 0:
                    a = jnp.where(2 * d < count, a, ghost)
                b_ = jnp.where(2 * d + 1 < entries, ghost, DUMMY)
                if 2 * d + 1 < K:
                    b_ = jnp.where(2 * d + 1 < count, lists_ref[2 * d + 1, t], b_)
                work_ref[n + d] = t * 65536 + a * 256 + b_
            n = n + lax.shift_right_logical(entries + 1, 1)
    for d in range(SIZES[0]):
        work_ref[n + d] = NT * 65536 + DUMMY
    work_ref[SLOTS - 1] = n
    if paired:
        ahead = jnp.minimum(without_ghosts, jnp.maximum(n - KEPT, 0))
        ahead = jnp.where(lower, jnp.minimum(lax.div(ahead, GROUP), EARLY), 0)
        work_ref[SLOTS - 2] = ahead * GROUP
        carry = (jnp.int32(-1), jnp.zeros((VROW, TILE), f32))
        interior_steps(0, ahead, GROUP, carry, work_ref, near16_ref, turned_ref, value16_ref, acc_ref)
    else:
        work_ref[SLOTS - 2] = 0


def interior_kernel(
    work_ref, near_ref, own_turned_ref, own_value_ref, before_ref, xa_ref, xb_ref, ya_ref, yb_ref,
    acc_ref, turned_ref, value_ref, far_ref, cut_ref,
):
    slots = []
    for axis, a_ref, b_ref in (("gx", xa_ref, xb_ref), ("gy", ya_ref, yb_ref)):
        even = jnp.bitwise_and(lax.axis_index(axis), 1) == 0
        a, b = ([ref[k] for k in range(8)] for ref in (a_ref, b_ref))
        if lax.axis_size(axis) == 2:
            slots.append(a)
        else:
            slots.append([jnp.where(even, q, p) for p, q in zip(a, b)])
            slots.append([jnp.where(even, p, q) for p, q in zip(a, b)])
    columns = [jnp.concatenate([slot[k] for slot in slots], axis=0) for k in range(8)]
    put_rows(far_ref, 0, far_rows(columns), NROW, NROW)
    put_rows(cut_ref, 0, value_rows(columns, columns[7]), VROW, VROW)
    @pl.when(work_ref[SLOTS - 2] > 0)
    def _():
        acc_ref[...] = before_ref[...]

    turned_ref[0 : GHOST * NROW, :] = own_turned_ref[...]
    value_ref[0 : GHOST * VROW, :] = own_value_ref[...]
    ghosts = len(slots) * FACE
    value_ref[GHOST * VROW : (GHOST + ghosts) * VROW, :] = cut_ref[0 : ghosts * VROW, :].astype(bf16)
    for b in range(ghosts // 4):
        turned_ref[GHOST * NROW + b * 128 : GHOST * NROW + (b + 1) * 128, :] = (
            far_ref[b * 128 : (b + 1) * 128, :].T.astype(bf16)
        )
    begin = work_ref[SLOTS - 2]
    left = work_ref[SLOTS - 1] - begin
    refs = (work_ref, near_ref, turned_ref, value_ref, acc_ref)
    before = lax.shift_right_logical(work_ref[jnp.maximum(begin - 1, 0)], 16)
    rows = pl.ds(pl.multiple_of(before * VROW, VROW), VROW)
    carry = (jnp.where(begin > 0, before, -1), before_ref[rows, :])
    for size in SIZES:
        steps = lax.div(left + (GROUP - 1 if size > GROUP else size - 1), size)
        carry = interior_steps(begin, steps, size, carry, *refs)
        begin, left = begin + steps * size, jnp.maximum(left - steps * size, 0)


def solved(total):
    return [total[c] / total[3] for c in range(3)]


def added(*terms):
    return [sum(values[1:], values[0]) for values in zip(*terms)]


def paired_slabs(parts_ref, beside_ref, across_ref):
    lower, inner = inner_outer()
    own, other = ([ref[4 + c] for c in range(4)] for ref in (parts_ref, beside_ref))
    mine_to, other_to = facing(lower, parts_ref), facing(lower, beside_ref)
    away = jnp.logical_not(lower)
    mine_from, other_from = facing(away, parts_ref), facing(away, beside_ref)
    summed, single = ([across_ref[k + c] for c in range(4)] for k in (0, 4))

    def chosen(first, second):
        return [jnp.where(inner, p, q) for p, q in zip(first, second)]

    here = solved(chosen(added(own, other_to, single), added(own, other_from)))
    near = solved(chosen(added(other, mine_from), added(other, mine_to, single)))
    past = solved(added(summed, mine_to))
    even = jnp.bitwise_and(lax.axis_index("gz"), 1) == 0
    below = [jnp.where(even, p, q) for p, q in zip(past, near)]
    above = [jnp.where(even, q, p) for p, q in zip(past, near)]
    return below, here, above


def ring_slabs(parts_ref, below_ref, above_ref, far_below_ref, far_above_ref):
    z, count = lax.axis_index("gz"), lax.axis_size("gz")

    def rows(ref, first):
        return [ref[first + c] for c in range(4)]

    def inside(flag, values, other=0.0):
        return [jnp.where(flag, value, other) for value in values]

    has_below, has_above = z >= 1, z <= count - 2
    here = added(rows(parts_ref, 4), inside(has_below, rows(below_ref, 0)), inside(has_above, rows(above_ref, 4)))
    below = added(
        inside(has_below, rows(below_ref, 4), 1.0), rows(parts_ref, 8), inside(z >= 2, rows(far_below_ref, 0))
    )
    above = added(
        inside(has_above, rows(above_ref, 0), 1.0), rows(parts_ref, 0), inside(z <= count - 3, rows(far_above_ref, 0))
    )
    return solved(below), solved(here), solved(above)


def update_kernel(paired, state_ref, cell_ref, acc_ref, parts_ref, *refs):
    slabs, refs = (refs[:2], refs[2:]) if paired else (refs[:4], refs[4:])
    new_ref, fluid_ref, table_ref = refs
    slab = parts_ref.shape[1]
    wide = 3 * slab
    first_row = (lax.axis_index("gz") - 1) * slab
    lower, here, upper = (paired_slabs if paired else ring_slabs)(parts_ref, *slabs)
    for c in range(3):
        fluid_ref[c] = here[c]
        table_ref[pl.ds(c * wide, slab), :] = lower[c]
        table_ref[pl.ds(c * wide + slab, slab), :] = here[c]
        table_ref[pl.ds(c * wide + 2 * slab, slab), :] = upper[c]

    def update_group(group, carry):
        rows = pl.ds(pl.multiple_of(group * 8, 8), 8)

        def sums(k):
            return acc_ref[pl.ds(group * 8 * VROW + k, 8, stride=VROW), :]

        weight = sums(9)
        cells = cell_ref[rows, :]
        high = lax.shift_right_logical(cells, 7) - first_row
        low = jnp.bitwise_and(cells, LANES - 1)
        at_cell = [jnp.zeros((8, LANES), f32)] * 3
        for h in range(wide):
            chosen = high == h
            for c in range(3):
                line = jnp.broadcast_to(table_ref[c * wide + h : c * wide + h + 1, :], (8, LANES))
                taken = jnp.take_along_axis(line, low, axis=1, mode="promise_in_bounds")
                at_cell[c] = jnp.where(chosen, taken, at_cell[c])
        r = state_ref[6, rows, :]
        ratio = r / radius_ref
        masses = ratio * ratio * ratio
        rate = drag_coef * r * r
        coupling = time_step * rate / masses
        for c in range(3):
            velocity = state_ref[3 + c, rows, :]
            lever = velocity - spring * centred(state_ref[c, rows, :])
            force = -damping * (lever * weight - (sums(c) + sums(3 + c) + sums(6 + c)))
            moved = velocity + time_step * force / masses
            new_ref[c, rows, :] = (moved + coupling * at_cell[c]) / (1.0 + coupling)
        return carry

    lax.fori_loop(0, NT // 8, update_group, 0, unroll=8)


def shifted(value, axis, steps):
    count = lax.axis_size(axis)
    return lax.ppermute(value, axis, [(i, (i + steps) % count) for i in range(count)])


def swapped(first, second, axis):
    count = lax.axis_size(axis)
    first = lax.ppermute(first, axis, [(i, i ^ 1) for i in range(count)])
    if count == 2:
        return first, first
    return first, lax.ppermute(second, axis, [(i, (i + (1 if i % 2 else -1)) % count) for i in range(count)])


vmem = pl.BlockSpec(memory_space=pltpu.VMEM)
hbm = pl.BlockSpec(memory_space=pltpu.HBM)
smem = pl.BlockSpec(memory_space=pltpu.SMEM)
roomy = pltpu.CompilerParams(vmem_limit_bytes=24 * 2**20)


def body(state, tile_lists, tile_counts, ghost_counts, cell_index, fluid_vel, fluid_frac):
    particles = state.shape[3]
    cell_count = fluid_vel.shape[3]
    slab = cell_count // LANES
    tiles = state.reshape(7, NT, TILE)
    cells = cell_index.reshape(NT, TILE)
    lists = tile_lists.reshape(NT, K).T
    counts = tile_counts.reshape(NT)
    ghosts = ghost_counts.reshape(4)

    def shape(*dims):
        return jax.ShapeDtypeStruct(dims, f32)

    def held(*values):
        return [pltpu.with_memory_space_constraint(value, pltpu.HBM) for value in values]

    face = shape(8, FACE, TILE)
    paired = lax.axis_size("gz") == 4
    parts, xa, xb, ya, yb, state_vmem, cells_vmem = pl.pallas_call(
        deposit_kernel,
        out_shape=(
            shape(12, slab, LANES), face, face, face, face,
            shape(7, NT, TILE), jax.ShapeDtypeStruct((NT, TILE), jnp.int32),
        ),
        in_specs=[hbm] * 5,
        out_specs=(vmem,) * 7,
        scratch_shapes=[
            pltpu.VMEM((3, slab, LANES), f32),
            pltpu.VMEM((slab, LANES), f32),
            pltpu.VMEM((8 * NT, TILE), f32),
            pltpu.VMEM((2, 12 * slab, LANES), f32),
            pltpu.VMEM((3 * slab, LANES), f32),
            pltpu.SMEM((4,), jnp.int32),
            pltpu.SemaphoreType.DMA((5,)),
        ],
        compiler_params=roomy,
        name="deposit",
    )(*held(tiles, cells, fluid_vel.reshape(3, slab, LANES), fluid_frac.reshape(slab, LANES), ghosts))

    if paired:
        beside = lax.ppermute(parts, "gz", [(i, i ^ 1) for i in range(4)])
        slabs = (beside,)
    else:
        slabs = (
            shifted(parts[0:8], "gz", 1), shifted(parts[4:12], "gz", -1),
            shifted(parts[0:4], "gz", 2), shifted(parts[8:12], "gz", -2),
        )
    ya, yb = swapped(ya, yb, "gy")
    xa, xb = swapped(xa, xb, "gx")

    near, turned, value, sums, work, *across = pl.pallas_call(
        functools.partial(feature_kernel, paired),
        out_shape=(
            jax.ShapeDtypeStruct((NT * 128 + 128, TILE), bf16),
            jax.ShapeDtypeStruct((GHOST * NROW, TILE), bf16),
            jax.ShapeDtypeStruct((GHOST * VROW, TILE), bf16),
            shape((NT + 1) * VROW, TILE),
            jax.ShapeDtypeStruct((SLOTS,), jnp.int32),
        ) + ((shape(8, slab, LANES),) if paired else ()),
        in_specs=[hbm] * 3 + [vmem] * (3 if paired else 1),
        out_specs=(vmem,) * 4 + (smem,) + ((vmem,) if paired else ()),
        scratch_shapes=[
            pltpu.VMEM((NT * NROW, TILE), f32),
            pltpu.VMEM((NT * NROW, TILE), f32),
            pltpu.VMEM((NT * VROW, TILE), f32),
            pltpu.SMEM((K, NT), jnp.int32),
            pltpu.SMEM((NT,), jnp.int32),
            pltpu.SMEM((4,), jnp.int32),
            pltpu.SemaphoreType.DMA((3,)),
        ],
        compiler_params=roomy,
        name="feature",
    )(*held(lists, counts, ghosts), state_vmem, *((parts, beside) if paired else ()))
    if paired:
        slabs += (lax.ppermute(across[0], "gz", [(i, i ^ 2) for i in range(4)]),)

    sums = pl.pallas_call(
        interior_kernel,
        out_shape=shape((NT + 1) * VROW, TILE),
        in_specs=[smem] + [vmem] * 8,
        out_specs=vmem,
        scratch_shapes=[
            pltpu.VMEM((NFAR * NROW, TILE), bf16),
            pltpu.VMEM((NFAR * VROW, TILE), bf16),
            pltpu.VMEM((4 * FACE * NROW, TILE), f32),
            pltpu.VMEM((4 * FACE * VROW, TILE), f32),
        ],
        compiler_params=roomy,
        name="interior",
    )(work, near, turned, value, sums, xa, xb, ya, yb)

    velocity_new, fluid_new = pl.pallas_call(
        functools.partial(update_kernel, paired),
        out_shape=(shape(3, NT, TILE), shape(3, slab, LANES)),
        in_specs=[vmem] * (4 + len(slabs)),
        out_specs=(vmem, vmem),
        scratch_shapes=[pltpu.VMEM((9 * slab, LANES), f32)],
        compiler_params=roomy,
        name="update",
    )(state_vmem, cells_vmem, sums, parts, *slabs)
    return velocity_new.reshape(3, 1, 1, particles), fluid_new.reshape(3, 1, 1, cell_count)


def solution(mesh):
    return jax.shard_map(
        body,
        mesh=mesh,
        in_specs=(
            P(None, "gx", "gy", "gz"),
            P("gx", "gy", "gz", None),
            P("gx", "gy", "gz"),
            P("gx", "gy", "gz", None),
            P("gx", "gy", "gz"),
            P(None, "gx", "gy", "gz"),
            P("gx", "gy", "gz"),
        ),
        out_specs=(P(None, "gx", "gy", "gz"), P(None, "gx", "gy", "gz")),
        check_vma=False,
    )
```

profile of v0, /device:TPU:0, one launch (start us, length us, event | category | flops | bytes accessed | tf_op | source)
XLA Modules:
  0.0 23.1 jit_solution(10455023488375118069)
XLA Ops:
  0.6 3.0 %deposit.1 = (f32[12,8,128]{2,1,0:T(8,128)S(1)}, f32[8,16,128]{2,1,0:T(8,128)S(1)}, f32[8,16,128]{2,1,0:T(8,128)S(1)}, f32[8,16,128]{2,1,0:T(8,128)S(1)}, f32[8,...) custom-call(f32[7,64,128]{2,1,0:T(8,128)} %bitcast.11, s32[64,128]{1,0:T(8,128)} %bitcast.12, ...), custom_call_target="tpu_custom_call" | custom-call | tf_op jit(solution)/shard_map/deposit/pallas_call | solution.py:474
  3.6 3.1 %collective-permute-start = (f32[12,8,128]{2,1,0:T(8,128)S(1)}, f32[12,8,128]{2,1,0:T(8,128)S(1)}, u32[]{:S(2)}, u32[]{:S(2)}) collective-permute-start(f32[12,8,128]{2,1,0:T(8,128)S(1)} %get-tuple-element.18.refs_0_.parts_ref), channel_id=1, source_target_pairs={{0,1},{1,0},{2,3},{3,2},{4,5},{5,4},{6,7},{7,6},{8,9},{9,8},{10,11... | collective-permute-start | bytes 147464 | tf_op jit(solution)/shard_map/ppermute | solution.py:496
  6.7 1.5 %collective-permute-start.1 = (f32[8,16,128]{2,1,0:T(8,128)S(1)}, f32[8,16,128]{2,1,0:T(8,128)S(1)}, u32[]{:S(2)}, u32[]{:S(2)}) collective-permute-start(f32[8,16,128]{2,1,0:T(8,128)S(1)} %get-tuple-element.24), channel_id=1, source_target_pairs={{0,8},{8,0},{16,24},{24,16},{1,9},{9,1},{17,25},{25,17},{2,10},{10... | collective-permute-start | bytes 196616 | tf_op jit(solution)/shard_map/ppermute | solution.py:444
  8.2 1.5 %collective-permute-start.2 = (f32[8,16,128]{2,1,0:T(8,128)S(1)}, f32[8,16,128]{2,1,0:T(8,128)S(1)}, u32[]{:S(2)}, u32[]{:S(2)}) collective-permute-start(f32[8,16,128]{2,1,0:T(8,128)S(1)} %get-tuple-element.25), channel_id=1, source_target_pairs={{0,24},{8,16},{16,8},{24,0},{1,25},{9,17},{17,9},{25,1},{2,26},{10... | collective-permute-start | bytes 196616 | tf_op jit(solution)/shard_map/ppermute | solution.py:447
  9.7 0.0 collective-permute-start.3
  9.7 0.0 collective-permute-done.refs_1_.refs_0_
  9.7 4.2 %feature.1 = (bf16[8320,128]{1,0:T(8,128)(2,1)S(1)}, bf16[2176,128]{1,0:T(8,128)(2,1)S(1)}, bf16[1088,128]{1,0:T(8,128)(2,1)S(1)}, f32[1040,128]{1,0:T(8,128)S(1...) custom-call(s32[8,64]{1,0:T(8,128)} %bitcast.15, s32[64]{0:T(128)} %bitcast.18, s32[4]{0:T(128)} %bitcast.17, ...), custom_call_target="tpu_custom_call" | custom-call | tf_op jit(solution)/shard_map/feature/pallas_call | solution.py:506
  13.8 1.0 %collective-permute-start.4 = (f32[8,8,128]{2,1,0:T(8,128)S(1)}, f32[8,8,128]{2,1,0:T(8,128)S(1)}, u32[]{:S(2)}, u32[]{:S(2)}) collective-permute-start(f32[8,8,128]{2,1,0:T(8,128)S(1)} %get-tuple-element.27), channel_id=1, source_target_pairs={{0,2},{1,3},{2,0},{3,1},{4,6},{5,7},{6,4},{7,5},{8,10},{9,11},{10,... | collective-permute-start | bytes 98312 | tf_op jit(solution)/shard_map/ppermute | solution.py:530
  14.9 0.0 collective-permute-done.1.xa_ref
  14.9 0.0 collective-permute-done.2.xb_ref
  14.9 0.0 collective-permute-done.3.ya_ref.yb_ref
  14.9 6.8 %interior.1.acc_ref = f32[1040,128]{1,0:T(8,128)S(1)} custom-call(s32[384]{0:T(512)S(1)} %get-tuple-element.19.work_ref, bf16[8320,128]{1,0:T(8,128)(2,1)S(1)} %get-tuple-element.20.near_ref, bf16[2176,128]{1,0:T(8,128)(2,1)S(1)} %get-tuple-element.21.own_turned_ref, bf16[1088,128]{1,0:T(8,128)(2,1)S(1)} %get-tuple-element.22.own_value_ref, ...), custom_call_target="tpu_custom_call" | custom-call | tf_op jit(solution)/shard_map/interior/pallas_call | solution.py:532
  21.7 0.0 collective-permute-done.4.refs_1_
  21.7 1.4 %update.1 = (f32[3,64,128]{2,1,0:T(8,128)}, f32[3,8,128]{2,1,0:T(8,128)}) custom-call(f32[7,64,128]{2,1,0:T(8,128)S(1)} %get-tuple-element.16.state_ref, s32[64,128]{1,0:T(8,128)S(1)} %get-tuple-element.17.cell_ref, f32[1040,128]{1,0:T(8,128)S(1)} %interior.1.acc_ref, f32[12,8,128]{2,1,0:T(8,128)S(1)} %get-tuple-element.18.refs_0_.parts_ref, ...), custom_call_target="tpu_custom_call" | custom-call | tf_op jit(solution)/shard_map/update/pallas_call | solution.py:547
Async XLA Ops:
  3.6 6.1 %collective-permute-start = (f32[12,8,128]{2,1,0:T(8,128)S(1)}, f32[12,8,128]{2,1,0:T(8,128)S(1)}, u32[]{:S(2)}, u32[]{:S(2)}) collective-permute-start(f32[12,8,128]{2,1,0:T(8,128)S(1)} %get-tuple-element.18.refs_0_.parts_ref), channel_id=1, source_target_pairs={{0,1},{1,0},{2,3},{3,2},{4,5},{5,4},{6,7},{7,6},{8,9},{9,8},{10,11... | collective-permute-start | bytes 147464 | tf_op jit(solution)/shard_map/ppermute | solution.py:496
  6.7 8.2 %collective-permute-start.1 = (f32[8,16,128]{2,1,0:T(8,128)S(1)}, f32[8,16,128]{2,1,0:T(8,128)S(1)}, u32[]{:S(2)}, u32[]{:S(2)}) collective-permute-start(f32[8,16,128]{2,1,0:T(8,128)S(1)} %get-tuple-element.24), channel_id=1, source_target_pairs={{0,8},{8,0},{16,24},{24,16},{1,9},{9,1},{17,25},{25,17},{2,10},{10... | collective-permute-start | bytes 196616 | tf_op jit(solution)/shard_map/ppermute | solution.py:444
  8.2 6.7 %collective-permute-start.2 = (f32[8,16,128]{2,1,0:T(8,128)S(1)}, f32[8,16,128]{2,1,0:T(8,128)S(1)}, u32[]{:S(2)}, u32[]{:S(2)}) collective-permute-start(f32[8,16,128]{2,1,0:T(8,128)S(1)} %get-tuple-element.25), channel_id=1, source_target_pairs={{0,24},{8,16},{16,8},{24,0},{1,25},{9,17},{17,9},{25,1},{2,26},{10... | collective-permute-start | bytes 196616 | tf_op jit(solution)/shard_map/ppermute | solution.py:447
  9.7 5.2 %collective-permute-start.3 = (f32[8,16,128]{2,1,0:T(8,128)S(1)}, f32[8,16,128]{2,1,0:T(8,128)S(1)}, u32[]{:S(2)}, u32[]{:S(2)}) collective-permute-start(f32[8,16,128]{2,1,0:T(8,128)S(1)} %get-tuple-element.26), channel_id=1, source_target_pairs={{0,4},{4,0},{1,5},{5,1},{2,6},{6,2},{3,7},{7,3},{8,12},{12,8},{9,1... | collective-permute-start | bytes 196616 | tf_op jit(solution)/shard_map/ppermute | solution.py:444
  13.8 7.8 %collective-permute-start.4 = (f32[8,8,128]{2,1,0:T(8,128)S(1)}, f32[8,8,128]{2,1,0:T(8,128)S(1)}, u32[]{:S(2)}, u32[]{:S(2)}) collective-permute-start(f32[8,8,128]{2,1,0:T(8,128)S(1)} %get-tuple-element.27), channel_id=1, source_target_pairs={{0,2},{1,3},{2,0},{3,1},{4,6},{5,7},{6,4},{7,5},{8,10},{9,11},{10,... | collective-permute-start | bytes 98312 | tf_op jit(solution)/shard_map/ppermute | solution.py:530
where the time goes:
time: 23.2 us; the launch traced here: 23.1 us
  Pallas kernels  15.3 us (66%)
  starting transfers between devices  7.1 us (31%)
  between operations  0.65 us (3%)
    pallas_call x1, Pallas kernels, body(): pl.pallas_call(interior_kernel, out_shape=shape((NT + 1) * VROW, TILE), i...  6.77 us
    pallas_call x1, Pallas kernels, body(): pl.pallas_call(functools.partial(feature_kernel, paired), out_shape=(jax....  4.16 us
    ppermute x1, starting transfers between devices, body(): beside = lax.ppermute(parts, 'gz', [(i, i ^ 1) for i in range(4)])  3.09 us
    pallas_call x1, Pallas kernels, body(): pl.pallas_call(deposit_kernel, out_shape=(shape(12, slab, LANES), face, f...  2.96 us
    ppermute x2, starting transfers between devices, swapped(): first = lax.ppermute(first, axis, [(i, i ^ 1) for i in range(count)])  1.49 us
    ppermute x1, starting transfers between devices, swapped(): lax.ppermute(second, axis, [(i, (i + (1 if i % 2 else -1)) % count) for i...  1.49 us
    pallas_call x1, Pallas kernels, body(): pl.pallas_call(functools.partial(update_kernel, paired), out_shape=(shape...  1.39 us
    ppermute x1, starting transfers between devices, body(): slabs += (lax.ppermute(across[0], 'gz', [(i, i ^ 2) for i in range(4)]),)  1.03 us
  transfers between devices with their start and end apart: 5, of which 0 were waited for; matrix products, arithmetic and copies ran while one was open for 0% of the time, Pallas kernels for 47%

commit v1 on v0

--- a/solution.py
+++ b/solution.py
@@ -33,8 +33,6 @@
 SIZES = (64, 32, 16)
 GROUP = 16
 EARLY = 2
-KEPT = 64
-SLOTS = NT * 6
 
 
 def parts_of(q):
@@ -100,7 +98,25 @@
     return both[:, :TILE] + both[:, TILE:]
 
 
-def interior_steps(begin, steps, size, carry, work_ref, near_ref, turned_ref, value_ref, acc_ref):
+def double_pair(k, d, lists_ref, counts_ref, faces_ref):
+    inside = k < NT
+    t = jnp.bitwise_and(k + 4 * GB, NT - 1)
+    face = lax.shift_right_logical(t * 171, 11)
+    place = t - face * GB
+    count = counts_ref[t]
+    entries = count + (place < faces_ref[face]).astype(jnp.int32)
+    ghost = faces_ref[8 + face] + place
+    at = 2 * d
+    first = jnp.where(at < count, lists_ref[jnp.minimum(at, K - 1), t], ghost)
+    second = jnp.where(
+        at + 1 < count, lists_ref[jnp.minimum(at + 1, K - 1), t], jnp.where(at + 1 < entries, ghost, DUMMY)
+    )
+    done = at + 2 >= entries
+    following = (k + done.astype(jnp.int32), jnp.where(done, 0, d + 1))
+    return jnp.where(inside, t, NT), jnp.where(inside, first, DUMMY), jnp.where(inside, second, DUMMY), following
+
+
+def interior_steps(steps, size, carry, tables, near_ref, turned_ref, value_ref, acc_ref):
     def near_block(t, s):
         start = t * 128 + 96 - NROW * jnp.bitwise_and(s, 3)
         return near_ref[pl.ds(pl.multiple_of(start, NROW), 128), :]
@@ -112,25 +128,22 @@
         return value_ref[pl.ds(pl.multiple_of(s * VROW, VROW), VROW), :]
 
     def step(group, carry):
+        (k, d), running = carry
         sums = []
-        for d in range(size):
-            word = work_ref[begin + group * size + d]
-            t = lax.shift_right_logical(word, 16)
-            a = jnp.bitwise_and(lax.shift_right_logical(word, 8), 255)
-            b = jnp.bitwise_and(word, 255)
+        for _ in range(size):
+            t, a, b, following = double_pair(k, d, *tables)
             near = jnp.minimum(t, NT - 1)
             total = pair_sums(
                 (far_block(a), far_block(b)),
                 (near_block(near, a), near_block(near, b)),
                 jnp.concatenate([value_block(a), value_block(b)], axis=1),
             )
-            sums.append((t, total))
-        last, running = carry
-        for t, total in sums:
-            running = total + jnp.where(t == last, running, 0.0)
+            sums.append((t, d, total))
+            k, d = following
+        for t, at, total in sums:
+            running = total + jnp.where(at > 0, running, 0.0)
             acc_ref[pl.ds(pl.multiple_of(t * VROW, VROW), VROW), :] = running
-            last = t
-        return last, running
+        return (k, d), running
 
     return lax.fori_loop(0, steps, step, carry)
 
@@ -233,14 +246,39 @@
     return slot_of, beside
 
 
-def feature_kernel(paired, lists_hbm, counts_hbm, ghost_hbm, state_ref, *refs):
+def put_faces(faces_ref, ghost_ref=None):
+    slot_of, beside = ghost_slots()
+    for face in range(8):
+        faces_ref[face] = jnp.where(beside[face], ghost_ref[face], 0) if ghost_ref is not None and face < 4 else 0
+        faces_ref[8 + face] = GHOST + slot_of[face] * FACE if face < 4 else DUMMY
+
+
+def early_words(without_ghosts):
+    if lax.axis_size("gz") != 4:
+        return jnp.int32(0)
+    return jnp.where(inner_outer()[0], GROUP * jnp.minimum(lax.div(without_ghosts, GROUP), EARLY), 0)
+
+
+def bare_words(counts_ref):
+    counts = [lax.shift_right_logical(counts_ref[t] + 1, 1) for t in range(4 * GB, NT)]
+    total = sum(counts)
+    early = early_words(total)
+    k, d, passed = jnp.int32(0), early, jnp.int32(0)
+    for place, count in enumerate(counts):
+        passed = passed + count
+        k = jnp.where(passed <= early, place + 1, k)
+        d = jnp.where(passed <= early, early - passed, d)
+    return total, early, (k, d)
+
+
+def feature_kernel(paired, lists_hbm, counts_hbm, state_ref, *refs):
     if paired:
         parts_ref, beside_ref, *refs = refs
-    near16_ref, turned_ref, value16_ref, acc_ref, work_ref, *refs = refs
+    near16_ref, turned_ref, value16_ref, acc_ref, *refs = refs
     if paired:
         across_ref, *refs = refs
-    near_ref, far_ref, value_ref, lists_ref, counts_ref, ghost_ref, sems = refs
-    copies = load([(lists_hbm, lists_ref), (counts_hbm, counts_ref), (ghost_hbm, ghost_ref)], sems)
+    near_ref, far_ref, value_ref, lists_ref, counts_ref, faces_ref, sems = refs
+    copies = load([(lists_hbm, lists_ref), (counts_hbm, counts_ref)], sems)
     if paired:
         lower, inner = inner_outer()
         mine, other = facing(lower, parts_ref), facing(lower, beside_ref)
@@ -255,55 +293,35 @@
     put_rows(near_ref, 0, near_rows(columns), NROW, NROW)
     put_rows(far_ref, 0, far_rows(columns), NROW, NROW)
     put_rows(value_ref, 0, value_rows(columns, jnp.ones((NT, TILE), f32)), VROW, VROW)
-    slot_of, beside = ghost_slots()
-    for copy in copies:
-        copy.wait()
-    alive = [jnp.where(beside[face], ghost_ref[face], 0) for face in range(4)]
-    n = jnp.int32(0)
-    for b in [*range(4 * GB // 4, NT // 4), *range(4 * GB // 4)]:
-        if b == 0:
-            without_ghosts = n
+    for b in range(NT // 4):
         rows = slice(b * 128, (b + 1) * 128)
         turned_ref[rows, :] = far_ref[rows, :].T.astype(bf16)
         rows = slice(b * 4 * VROW, (b + 1) * 4 * VROW)
         value16_ref[rows, :] = value_ref[rows, :].astype(bf16)
-        for t in range(4 * b, 4 * b + 4):
-            near16_ref[t * 128 : (t + 1) * 128, :] = jnp.concatenate(
-                [jnp.zeros((96, TILE), bf16), near_ref[t * NROW : (t + 1) * NROW, :].astype(bf16)], axis=0
+    for t in range(NT):
+        near16_ref[t * 128 : (t + 1) * 128, :] = jnp.concatenate(
+            [jnp.zeros((96, TILE), bf16), near_ref[t * NROW : (t + 1) * NROW, :].astype(bf16)], axis=0
+        )
+    for copy in copies:
+        copy.wait()
+    if paired:
+        @pl.when(lower)
+        def _():
+            put_faces(faces_ref)
+            _, words, _ = bare_words(counts_ref)
+            carry = ((jnp.int32(0), jnp.int32(0)), jnp.zeros((VROW, TILE), f32))
+            tables = (lists_ref, counts_ref, faces_ref)
+            interior_steps(
+                lax.div(words, GROUP), GROUP, carry, tables, near16_ref, turned_ref, value16_ref, acc_ref
             )
-            count = counts_ref[t]
-            face, place = t // GB, t % GB
-            if face < 4:
-                ghost = GHOST + slot_of[face] * FACE + place
-                entries = count + (place < alive[face]).astype(jnp.int32)
-            else:
-                ghost, entries = DUMMY, count
-            for d in range((K + 1 + (face < 4)) // 2):
-                a = lists_ref[min(2 * d, K - 1), t]
-                if face < 4 and d > 0:
-                    a = jnp.where(2 * d < count, a, ghost)
-                b_ = jnp.where(2 * d + 1 < entries, ghost, DUMMY)
-                if 2 * d + 1 < K:
-                    b_ = jnp.where(2 * d + 1 < count, lists_ref[2 * d + 1, t], b_)
-                work_ref[n + d] = t * 65536 + a * 256 + b_
-            n = n + lax.shift_right_logical(entries + 1, 1)
-    for d in range(SIZES[0]):
-        work_ref[n + d] = NT * 65536 + DUMMY
-    work_ref[SLOTS - 1] = n
-    if paired:
-        ahead = jnp.minimum(without_ghosts, jnp.maximum(n - KEPT, 0))
-        ahead = jnp.where(lower, jnp.minimum(lax.div(ahead, GROUP), EARLY), 0)
-        work_ref[SLOTS - 2] = ahead * GROUP
-        carry = (jnp.int32(-1), jnp.zeros((VROW, TILE), f32))
-        interior_steps(0, ahead, GROUP, carry, work_ref, near16_ref, turned_ref, value16_ref, acc_ref)
-    else:
-        work_ref[SLOTS - 2] = 0
 
 
 def interior_kernel(
-    work_ref, near_ref, own_turned_ref, own_value_ref, before_ref, xa_ref, xb_ref, ya_ref, yb_ref,
-    acc_ref, turned_ref, value_ref, far_ref, cut_ref,
+    lists_hbm, counts_hbm, ghost_hbm, near_ref, own_turned_ref, own_value_ref, before_ref,
+    xa_ref, xb_ref, ya_ref, yb_ref,
+    acc_ref, turned_ref, value_ref, far_ref, cut_ref, lists_ref, counts_ref, ghost_ref, faces_ref, sems,
 ):
+    copies = load([(lists_hbm, lists_ref), (counts_hbm, counts_ref), (ghost_hbm, ghost_ref)], sems)
     slots = []
     for axis, a_ref, b_ref in (("gx", xa_ref, xb_ref), ("gy", ya_ref, yb_ref)):
         even = jnp.bitwise_and(lax.axis_index(axis), 1) == 0
@@ -316,10 +334,6 @@
     columns = [jnp.concatenate([slot[k] for slot in slots], axis=0) for k in range(8)]
     put_rows(far_ref, 0, far_rows(columns), NROW, NROW)
     put_rows(cut_ref, 0, value_rows(columns, columns[7]), VROW, VROW)
-    @pl.when(work_ref[SLOTS - 2] > 0)
-    def _():
-        acc_ref[...] = before_ref[...]
-
     turned_ref[0 : GHOST * NROW, :] = own_turned_ref[...]
     value_ref[0 : GHOST * VROW, :] = own_value_ref[...]
     ghosts = len(slots) * FACE
@@ -328,16 +342,27 @@
         turned_ref[GHOST * NROW + b * 128 : GHOST * NROW + (b + 1) * 128, :] = (
             far_ref[b * 128 : (b + 1) * 128, :].T.astype(bf16)
         )
-    begin = work_ref[SLOTS - 2]
-    left = work_ref[SLOTS - 1] - begin
-    refs = (work_ref, near_ref, turned_ref, value_ref, acc_ref)
-    before = lax.shift_right_logical(work_ref[jnp.maximum(begin - 1, 0)], 16)
-    rows = pl.ds(pl.multiple_of(before * VROW, VROW), VROW)
-    carry = (jnp.where(begin > 0, before, -1), before_ref[rows, :])
+    for copy in copies:
+        copy.wait()
+    put_faces(faces_ref, ghost_ref)
+    bare, begin, place = bare_words(counts_ref)
+    left = bare - begin
+    for t in range(4 * GB):
+        ghost = (t % GB < faces_ref[t // GB]).astype(jnp.int32)
+        left = left + lax.shift_right_logical(counts_ref[t] + ghost + 1, 1)
+
+    @pl.when(begin > 0)
+    def _():
+        rows = slice(4 * GB * VROW, NT * VROW)
+        acc_ref[rows, :] = before_ref[rows, :]
+
+    tile = jnp.bitwise_and(place[0] + 4 * GB, NT - 1)
+    carry = (place, before_ref[pl.ds(pl.multiple_of(tile * VROW, VROW), VROW), :])
+    tables = (lists_ref, counts_ref, faces_ref)
     for size in SIZES:
         steps = lax.div(left + (GROUP - 1 if size > GROUP else size - 1), size)
-        carry = interior_steps(begin, steps, size, carry, *refs)
-        begin, left = begin + steps * size, jnp.maximum(left - steps * size, 0)
+        carry = interior_steps(steps, size, carry, tables, near_ref, turned_ref, value_ref, acc_ref)
+        left = jnp.maximum(left - steps * size, 0)
 
 
 def solved(total):
@@ -449,7 +474,6 @@
 
 vmem = pl.BlockSpec(memory_space=pltpu.VMEM)
 hbm = pl.BlockSpec(memory_space=pltpu.HBM)
-smem = pl.BlockSpec(memory_space=pltpu.SMEM)
 roomy = pltpu.CompilerParams(vmem_limit_bytes=24 * 2**20)
 
 
@@ -503,46 +527,50 @@
     ya, yb = swapped(ya, yb, "gy")
     xa, xb = swapped(xa, xb, "gx")
 
-    near, turned, value, sums, work, *across = pl.pallas_call(
+    near, turned, value, sums, *across = pl.pallas_call(
         functools.partial(feature_kernel, paired),
         out_shape=(
             jax.ShapeDtypeStruct((NT * 128 + 128, TILE), bf16),
             jax.ShapeDtypeStruct((GHOST * NROW, TILE), bf16),
             jax.ShapeDtypeStruct((GHOST * VROW, TILE), bf16),
             shape((NT + 1) * VROW, TILE),
-            jax.ShapeDtypeStruct((SLOTS,), jnp.int32),
         ) + ((shape(8, slab, LANES),) if paired else ()),
-        in_specs=[hbm] * 3 + [vmem] * (3 if paired else 1),
-        out_specs=(vmem,) * 4 + (smem,) + ((vmem,) if paired else ()),
+        in_specs=[hbm] * 2 + [vmem] * (3 if paired else 1),
+        out_specs=(vmem,) * (5 if paired else 4),
         scratch_shapes=[
             pltpu.VMEM((NT * NROW, TILE), f32),
             pltpu.VMEM((NT * NROW, TILE), f32),
             pltpu.VMEM((NT * VROW, TILE), f32),
             pltpu.SMEM((K, NT), jnp.int32),
             pltpu.SMEM((NT,), jnp.int32),
-            pltpu.SMEM((4,), jnp.int32),
-            pltpu.SemaphoreType.DMA((3,)),
+            pltpu.SMEM((16,), jnp.int32),
+            pltpu.SemaphoreType.DMA((2,)),
         ],
         compiler_params=roomy,
         name="feature",
-    )(*held(lists, counts, ghosts), state_vmem, *((parts, beside) if paired else ()))
+    )(*held(lists, counts), state_vmem, *((parts, beside) if paired else ()))
     if paired:
         slabs += (lax.ppermute(across[0], "gz", [(i, i ^ 2) for i in range(4)]),)
 
     sums = pl.pallas_call(
         interior_kernel,
         out_shape=shape((NT + 1) * VROW, TILE),
-        in_specs=[smem] + [vmem] * 8,
+        in_specs=[hbm] * 3 + [vmem] * 8,
         out_specs=vmem,
         scratch_shapes=[
             pltpu.VMEM((NFAR * NROW, TILE), bf16),
             pltpu.VMEM((NFAR * VROW, TILE), bf16),
             pltpu.VMEM((4 * FACE * NROW, TILE), f32),
             pltpu.VMEM((4 * FACE * VROW, TILE), f32),
+            pltpu.SMEM((K, NT), jnp.int32),
+            pltpu.SMEM((NT,), jnp.int32),
+            pltpu.SMEM((4,), jnp.int32),
+            pltpu.SMEM((16,), jnp.int32),
+            pltpu.SemaphoreType.DMA((3,)),
         ],
         compiler_params=roomy,
         name="interior",
-    )(work, near, turned, value, sums, xa, xb, ya, yb)
+    )(*held(lists, counts, ghosts), near, turned, value, sums, xa, xb, ya, yb)
 
     velocity_new, fluid_new = pl.pallas_call(
         functools.partial(update_kernel, paired),

time: 23.2 us -> 21.9 us (0.944)
  Pallas kernels: 15.3 us -> 13.8 us
    pallas_call x1, Pallas kernels: 4.16 us -> 2.54 us  [body(): pl.pallas_call(functools.partial(feature_kernel, paired), out_shape=(jax....]
  transfers between devices with their start and end apart: 5 -> 5, of which waited for: 0 -> 1; matrix products, arithmetic and copies ran while one was open for 0% -> 0% of each run, Pallas kernels for 47% -> 44%
where the time goes in v1:
time: 21.9 us; the launch traced here: 21.7 us
  Pallas kernels  13.8 us (63%)
  starting transfers between devices  7.06 us (32%)
  between operations  0.67 us (3%)
    pallas_call x1, Pallas kernels, body(): pl.pallas_call(interior_kernel, out_shape=shape((NT + 1) * VROW, TILE), i...  6.98 us
    ppermute x1, starting transfers between devices, body(): beside = lax.ppermute(parts, 'gz', [(i, i ^ 1) for i in range(4)])  3.09 us
    pallas_call x1, Pallas kernels, body(): pl.pallas_call(deposit_kernel, out_shape=(shape(12, slab, LANES), face, f...  2.96 us
    pallas_call x1, Pallas kernels, body(): pl.pallas_call(functools.partial(feature_kernel, paired), out_shape=(jax....  2.54 us
    ppermute x2, starting transfers between devices, swapped(): first = lax.ppermute(first, axis, [(i, i ^ 1) for i in range(count)])  1.49 us
    ppermute x1, starting transfers between devices, swapped(): lax.ppermute(second, axis, [(i, (i + (1 if i % 2 else -1)) % count) for i...  1.49 us
    pallas_call x1, Pallas kernels, body(): pl.pallas_call(functools.partial(update_kernel, paired), out_shape=(shape...  1.37 us
    ppermute x1, starting transfers between devices, body(): slabs += (lax.ppermute(across[0], 'gz', [(i, i ^ 2) for i in range(4)]),)  0.98 us
  transfers between devices with their start and end apart: 5, of which 1 were waited for; matrix products, arithmetic and copies ran while one was open for 0% of the time, Pallas kernels for 44%

profile of v1, /device:TPU:0, one launch (start us, length us, event | category | flops | bytes accessed | tf_op | source)
XLA Modules:
  0.0 21.7 jit_solution(17879975746475451416)
XLA Ops:
  0.6 3.0 %deposit.1 = (f32[12,8,128]{2,1,0:T(8,128)S(1)}, f32[8,16,128]{2,1,0:T(8,128)S(1)}, f32[8,16,128]{2,1,0:T(8,128)S(1)}, f32[8,16,128]{2,1,0:T(8,128)S(1)}, f32[8,...) custom-call(f32[7,64,128]{2,1,0:T(8,128)} %bitcast.11, s32[64,128]{1,0:T(8,128)} %bitcast.12, ...), custom_call_target="tpu_custom_call" | custom-call | tf_op jit(solution)/shard_map/deposit/pallas_call | solution.py:498
  3.6 3.1 %collective-permute-start = (f32[12,8,128]{2,1,0:T(8,128)S(1)}, f32[12,8,128]{2,1,0:T(8,128)S(1)}, u32[]{:S(2)}, u32[]{:S(2)}) collective-permute-start(f32[12,8,128]{2,1,0:T(8,128)S(1)} %get-tuple-element.17.refs_0_.parts_ref), channel_id=1, source_target_pairs={{0,1},{1,0},{2,3},{3,2},{4,5},{5,4},{6,7},{7,6},{8,9},{9,8},{10,11... | collective-permute-start | bytes 147464 | tf_op jit(solution)/shard_map/ppermute | solution.py:520
  6.7 1.5 %collective-permute-start.1 = (f32[8,16,128]{2,1,0:T(8,128)S(1)}, f32[8,16,128]{2,1,0:T(8,128)S(1)}, u32[]{:S(2)}, u32[]{:S(2)}) collective-permute-start(f32[8,16,128]{2,1,0:T(8,128)S(1)} %get-tuple-element.22), channel_id=1, source_target_pairs={{0,8},{8,0},{16,24},{24,16},{1,9},{9,1},{17,25},{25,17},{2,10},{10... | collective-permute-start | bytes 196616 | tf_op jit(solution)/shard_map/ppermute | solution.py:469
  8.2 1.5 %collective-permute-start.2 = (f32[8,16,128]{2,1,0:T(8,128)S(1)}, f32[8,16,128]{2,1,0:T(8,128)S(1)}, u32[]{:S(2)}, u32[]{:S(2)}) collective-permute-start(f32[8,16,128]{2,1,0:T(8,128)S(1)} %get-tuple-element.23), channel_id=1, source_target_pairs={{0,24},{8,16},{16,8},{24,0},{1,25},{9,17},{17,9},{25,1},{2,26},{10... | collective-permute-start | bytes 196616 | tf_op jit(solution)/shard_map/ppermute | solution.py:472
  9.7 0.0 collective-permute-start.3
  9.7 0.0 collective-permute-done.refs_1_.refs_0_
  9.7 2.5 %feature.1 = (bf16[8320,128]{1,0:T(8,128)(2,1)S(1)}, bf16[2176,128]{1,0:T(8,128)(2,1)S(1)}, bf16[1088,128]{1,0:T(8,128)(2,1)S(1)}, f32[1040,128]{1,0:T(8,128)S(1)}, f32[8,8,128]{2,1,0:T(8,128)S(1)}) custom-call(s32[8,64]{1,0:T(8,128)} %bitcast.13, s32[64]{0:T(128)} %bitcast.19, f32[7,64,128]{2,1,0:T(8,128)S(1)} %get-tuple-element.15.state_ref, ...), custom_call_target="tpu_custom_call" | custom-call | tf_op jit(solution)/shard_map/feature/pallas_call | solution.py:530
  12.2 1.0 %collective-permute-start.4 = (f32[8,8,128]{2,1,0:T(8,128)S(1)}, f32[8,8,128]{2,1,0:T(8,128)S(1)}, u32[]{:S(2)}, u32[]{:S(2)}) collective-permute-start(f32[8,8,128]{2,1,0:T(8,128)S(1)} %get-tuple-element.25), channel_id=1, source_target_pairs={{0,2},{1,3},{2,0},{3,1},{4,6},{5,7},{6,4},{7,5},{8,10},{9,11},{10,... | collective-permute-start | bytes 98312 | tf_op jit(solution)/shard_map/ppermute | solution.py:553
  13.2 0.0 collective-permute-done.1.xa_ref
  13.2 0.1 collective-permute-done.2.xb_ref
  13.3 0.0 collective-permute-done.3.ya_ref.yb_ref
  13.3 7.0 %interior.1.acc_ref = f32[1040,128]{1,0:T(8,128)S(1)} custom-call(s32[8,64]{1,0:T(8,128)} %bitcast.14, s32[64]{0:T(128)} %bitcast.20, s32[4]{0:T(128)} %bitcast.18, bf16[8320,128]{1,0:T(8,128)(2,1)S(1)} %get-tuple-element.18.near_ref, bf16[2176,128]{1,0:T(8,128)(2,1)S(1)} %get-tuple-element.19.own_turned_ref, ...), custom_call_target="tpu_custom_call" | custom-call | tf_op jit(solution)/shard_map/interior/pallas_call | solution.py:555
  20.3 0.0 collective-permute-done.4.refs_1_
  20.3 1.4 %update.1 = (f32[3,64,128]{2,1,0:T(8,128)}, f32[3,8,128]{2,1,0:T(8,128)}) custom-call(f32[7,64,128]{2,1,0:T(8,128)S(1)} %get-tuple-element.15.state_ref, s32[64,128]{1,0:T(8,128)S(1)} %get-tuple-element.16.cell_ref, f32[1040,128]{1,0:T(8,128)S(1)} %interior.1.acc_ref, f32[12,8,128]{2,1,0:T(8,128)S(1)} %get-tuple-element.17.refs_0_.parts_ref, ...), custom_call_target="tpu_custom_call" | custom-call | tf_op jit(solution)/shard_map/update/pallas_call | solution.py:575
Async XLA Ops:
  3.6 6.1 %collective-permute-start = (f32[12,8,128]{2,1,0:T(8,128)S(1)}, f32[12,8,128]{2,1,0:T(8,128)S(1)}, u32[]{:S(2)}, u32[]{:S(2)}) collective-permute-start(f32[12,8,128]{2,1,0:T(8,128)S(1)} %get-tuple-element.17.refs_0_.parts_ref), channel_id=1, source_target_pairs={{0,1},{1,0},{2,3},{3,2},{4,5},{5,4},{6,7},{7,6},{8,9},{9,8},{10,11... | collective-permute-start | bytes 147464 | tf_op jit(solution)/shard_map/ppermute | solution.py:520
  6.7 6.5 %collective-permute-start.1 = (f32[8,16,128]{2,1,0:T(8,128)S(1)}, f32[8,16,128]{2,1,0:T(8,128)S(1)}, u32[]{:S(2)}, u32[]{:S(2)}) collective-permute-start(f32[8,16,128]{2,1,0:T(8,128)S(1)} %get-tuple-element.22), channel_id=1, source_target_pairs={{0,8},{8,0},{16,24},{24,16},{1,9},{9,1},{17,25},{25,17},{2,10},{10... | collective-permute-start | bytes 196616 | tf_op jit(solution)/shard_map/ppermute | solution.py:469
  8.2 5.2 %collective-permute-start.2 = (f32[8,16,128]{2,1,0:T(8,128)S(1)}, f32[8,16,128]{2,1,0:T(8,128)S(1)}, u32[]{:S(2)}, u32[]{:S(2)}) collective-permute-start(f32[8,16,128]{2,1,0:T(8,128)S(1)} %get-tuple-element.23), channel_id=1, source_target_pairs={{0,24},{8,16},{16,8},{24,0},{1,25},{9,17},{17,9},{25,1},{2,26},{10... | collective-permute-start | bytes 196616 | tf_op jit(solution)/shard_map/ppermute | solution.py:472
  9.7 3.7 %collective-permute-start.3 = (f32[8,16,128]{2,1,0:T(8,128)S(1)}, f32[8,16,128]{2,1,0:T(8,128)S(1)}, u32[]{:S(2)}, u32[]{:S(2)}) collective-permute-start(f32[8,16,128]{2,1,0:T(8,128)S(1)} %get-tuple-element.24), channel_id=1, source_target_pairs={{0,4},{4,0},{1,5},{5,1},{2,6},{6,2},{3,7},{7,3},{8,12},{12,8},{9,1... | collective-permute-start | bytes 196616 | tf_op jit(solution)/shard_map/ppermute | solution.py:469
  12.2 8.1 %collective-permute-start.4 = (f32[8,8,128]{2,1,0:T(8,128)S(1)}, f32[8,8,128]{2,1,0:T(8,128)S(1)}, u32[]{:S(2)}, u32[]{:S(2)}) collective-permute-start(f32[8,8,128]{2,1,0:T(8,128)S(1)} %get-tuple-element.25), channel_id=1, source_target_pairs={{0,2},{1,3},{2,0},{3,1},{4,6},{5,7},{6,4},{7,5},{8,10},{9,11},{10,... | collective-permute-start | bytes 98312 | tf_op jit(solution)/shard_map/ppermute | solution.py:553

commit v2 on v1

--- a/solution.py
+++ b/solution.py
@@ -32,7 +32,7 @@
 NFAR = GHOST + 4 * FACE
 SIZES = (64, 32, 16)
 GROUP = 16
-EARLY = 2
+EARLY = (32, 8)
 
 
 def parts_of(q):
@@ -256,7 +256,10 @@
 def early_words(without_ghosts):
     if lax.axis_size("gz") != 4:
         return jnp.int32(0)
-    return jnp.where(inner_outer()[0], GROUP * jnp.minimum(lax.div(without_ghosts, GROUP), EARLY), 0)
+    words = jnp.int32(0)
+    for size in EARLY:
+        words = words + jnp.where(without_ghosts - words >= size, size, 0)
+    return jnp.where(inner_outer()[0], words, 0)
 
 
 def bare_words(counts_ref):
@@ -311,9 +314,12 @@
             _, words, _ = bare_words(counts_ref)
             carry = ((jnp.int32(0), jnp.int32(0)), jnp.zeros((VROW, TILE), f32))
             tables = (lists_ref, counts_ref, faces_ref)
-            interior_steps(
-                lax.div(words, GROUP), GROUP, carry, tables, near16_ref, turned_ref, value16_ref, acc_ref
-            )
+            for size in EARLY:
+                steps = (words >= size).astype(jnp.int32)
+                carry = interior_steps(
+                    steps, size, carry, tables, near16_ref, turned_ref, value16_ref, acc_ref
+                )
+                words = words - steps * size
 
 
 def interior_kernel(
@@ -464,12 +470,23 @@
     return lax.ppermute(value, axis, [(i, (i + steps) % count) for i in range(count)])
 
 
-def swapped(first, second, axis):
+def rung(first, second, axis):
     count = lax.axis_size(axis)
     first = lax.ppermute(first, axis, [(i, i ^ 1) for i in range(count)])
-    if count == 2:
-        return first, first
     return first, lax.ppermute(second, axis, [(i, (i + (1 if i % 2 else -1)) % count) for i in range(count)])
+
+
+def swapped(first, second, axis, core):
+    count = lax.axis_size(axis)
+    first = lax.ppermute(first, axis, [(i, i ^ 1) for i in range(count)])
+    cores = lax.axis_size(core)
+    pairs = []
+    for i in range(count):
+        partner = i + 1 if i % 2 else i - 1
+        for c in range(cores):
+            to = (partner, c) if 0 <= partner < count else (i, c ^ 1)
+            pairs.append((i * cores + c, to[0] * cores + to[1]))
+    return first, lax.ppermute(second, (axis, core), pairs)
 
 
 vmem = pl.BlockSpec(memory_space=pltpu.VMEM)
@@ -524,8 +541,11 @@
             shifted(parts[0:8], "gz", 1), shifted(parts[4:12], "gz", -1),
             shifted(parts[0:4], "gz", 2), shifted(parts[8:12], "gz", -2),
         )
-    ya, yb = swapped(ya, yb, "gy")
-    xa, xb = swapped(xa, xb, "gx")
+    if lax.axis_size("gy") == 2:
+        ya = yb = lax.ppermute(ya, "gy", [(0, 1), (1, 0)])
+    else:
+        ya, yb = rung(ya, yb, "gy")
+    xa, xb = swapped(xa, xb, "gx", "gy")
 
     near, turned, value, sums, *across = pl.pallas_call(
         functools.partial(feature_kernel, paired),

time: 21.9 us -> 21.4 us (0.977)
  starting transfers between devices: 7.06 us -> 6.23 us
  Pallas kernels: 13.8 us -> 14.1 us
    ppermute x1 -> x2, starting transfers between devices: 1.49 us -> 0.51 us  [the longest x1 0.51 us: body(): ya = yb = lax.ppermute(ya, 'gy', [(0, 1), (1, 0)])]
    pallas_call x1, Pallas kernels: 2.54 us -> 2.82 us  [body(): pl.pallas_call(functools.partial(feature_kernel, paired), out_shape=(jax....]
    ppermute x2 -> x1, starting transfers between devices: 1.49 us -> 1.49 us  [swapped(): first = lax.ppermute(first, axis, [(i, i ^ 1) for i in range(count)])]
  transfers between devices with their start and end apart: 5 -> 5, of which waited for: 1 -> 1; matrix products, arithmetic and copies ran while one was open for 0% -> 0% of each run, Pallas kernels for 44% -> 46%
where the time goes in v2:
time: 21.4 us; the launch traced here: 21.1 us
  Pallas kernels  14.1 us (66%)
  starting transfers between devices  6.23 us (29%)
  between operations  0.67 us (3%)
    pallas_call x1, Pallas kernels, body(): pl.pallas_call(interior_kernel, out_shape=shape((NT + 1) * VROW, TILE), i...  6.98 us
    ppermute x1, starting transfers between devices, body(): beside = lax.ppermute(parts, 'gz', [(i, i ^ 1) for i in range(4)])  3.09 us
    pallas_call x1, Pallas kernels, body(): pl.pallas_call(deposit_kernel, out_shape=(shape(12, slab, LANES), face, f...  2.96 us
    pallas_call x1, Pallas kernels, body(): pl.pallas_call(functools.partial(feature_kernel, paired), out_shape=(jax....  2.82 us
    ppermute x1, starting transfers between devices, swapped(): first = lax.ppermute(first, axis, [(i, i ^ 1) for i in range(count)])  1.49 us
    pallas_call x1, Pallas kernels, body(): pl.pallas_call(functools.partial(update_kernel, paired), out_shape=(shape...  1.37 us
    ppermute x1, starting transfers between devices, body(): slabs += (lax.ppermute(across[0], 'gz', [(i, i ^ 2) for i in range(4)]),)  1.14 us
    ppermute x1, starting transfers between devices, body(): ya = yb = lax.ppermute(ya, 'gy', [(0, 1), (1, 0)])  0.51 us
  transfers between devices with their start and end apart: 5, of which 1 were waited for; matrix products, arithmetic and copies ran while one was open for 0% of the time, Pallas kernels for 46%

profile of v2, /device:TPU:0, one launch (start us, length us, event | category | flops | bytes accessed | tf_op | source)
XLA Modules:
  0.0 21.1 jit_solution(7519387960383256029)
XLA Ops:
  0.6 3.0 %deposit.1 = (f32[12,8,128]{2,1,0:T(8,128)S(1)}, f32[8,16,128]{2,1,0:T(8,128)S(1)}, f32[8,16,128]{2,1,0:T(8,128)S(1)}, f32[8,16,128]{2,1,0:T(8,128)S(1)}, f32[8,...) custom-call(f32[7,64,128]{2,1,0:T(8,128)} %bitcast.11, s32[64,128]{1,0:T(8,128)} %bitcast.12, ...), custom_call_target="tpu_custom_call" | custom-call | tf_op jit(solution)/shard_map/deposit/pallas_call | solution.py:515
  3.6 3.1 %collective-permute-start = (f32[12,8,128]{2,1,0:T(8,128)S(1)}, f32[12,8,128]{2,1,0:T(8,128)S(1)}, u32[]{:S(2)}, u32[]{:S(2)}) collective-permute-start(f32[12,8,128]{2,1,0:T(8,128)S(1)} %get-tuple-element.17.refs_0_.parts_ref), channel_id=1, source_target_pairs={{0,1},{1,0},{2,3},{3,2},{4,5},{5,4},{6,7},{7,6},{8,9},{9,8},{10,11... | collective-permute-start | bytes 147464 | tf_op jit(solution)/shard_map/ppermute | solution.py:537
  6.7 1.5 %collective-permute-start.1 = (f32[8,16,128]{2,1,0:T(8,128)S(1)}, f32[8,16,128]{2,1,0:T(8,128)S(1)}, u32[]{:S(2)}, u32[]{:S(2)}) collective-permute-start(f32[8,16,128]{2,1,0:T(8,128)S(1)} %get-tuple-element.22), channel_id=1, source_target_pairs={{0,8},{8,0},{16,24},{24,16},{1,9},{9,1},{17,25},{25,17},{2,10},{10... | collective-permute-start | bytes 196616 | tf_op jit(solution)/shard_map/ppermute | solution.py:481
  8.2 0.0 collective-permute-start.2
  8.2 0.5 %collective-permute-start.3 = (f32[8,16,128]{2,1,0:T(8,128)S(1)}, f32[8,16,128]{2,1,0:T(8,128)S(1)}, u32[]{:S(2)}, u32[]{:S(2)}) collective-permute-start(f32[8,16,128]{2,1,0:T(8,128)S(1)} %get-tuple-element.24), channel_id=1, source_target_pairs={{0,4},{4,0},{1,5},{5,1},{2,6},{6,2},{3,7},{7,3},{8,12},{12,8},{9,1... | collective-permute-start | bytes 196616 | tf_op jit(solution)/shard_map/ppermute | solution.py:545
  8.7 0.1 collective-permute-done.refs_1_.refs_0_
  8.8 2.8 %feature.1 = (bf16[8320,128]{1,0:T(8,128)(2,1)S(1)}, bf16[2176,128]{1,0:T(8,128)(2,1)S(1)}, bf16[1088,128]{1,0:T(8,128)(2,1)S(1)}, f32[1040,128]{1,0:T(8,128)S(1)}, f32[8,8,128]{2,1,0:T(8,128)S(1)}) custom-call(s32[8,64]{1,0:T(8,128)} %bitcast.13, s32[64]{0:T(128)} %bitcast.19, f32[7,64,128]{2,1,0:T(8,128)S(1)} %get-tuple-element.15.state_ref, ...), custom_call_target="tpu_custom_call" | custom-call | tf_op jit(solution)/shard_map/feature/pallas_call | solution.py:550
  11.6 1.1 %collective-permute-start.4 = (f32[8,8,128]{2,1,0:T(8,128)S(1)}, f32[8,8,128]{2,1,0:T(8,128)S(1)}, u32[]{:S(2)}, u32[]{:S(2)}) collective-permute-start(f32[8,8,128]{2,1,0:T(8,128)S(1)} %get-tuple-element.25), channel_id=1, source_target_pairs={{0,2},{1,3},{2,0},{3,1},{4,6},{5,7},{6,4},{7,5},{8,10},{9,11},{10,... | collective-permute-start | bytes 98312 | tf_op jit(solution)/shard_map/ppermute | solution.py:573
  12.7 0.0 collective-permute-done.1.xa_ref
  12.7 0.0 collective-permute-done.2.xb_ref
  12.7 0.0 collective-permute-done.3.ya_ref.yb_ref
  12.7 7.0 %interior.1.acc_ref = f32[1040,128]{1,0:T(8,128)S(1)} custom-call(s32[8,64]{1,0:T(8,128)} %bitcast.14, s32[64]{0:T(128)} %bitcast.20, s32[4]{0:T(128)} %bitcast.18, bf16[8320,128]{1,0:T(8,128)(2,1)S(1)} %get-tuple-element.18.near_ref, bf16[2176,128]{1,0:T(8,128)(2,1)S(1)} %get-tuple-element.19.own_turned_ref, ...), custom_call_target="tpu_custom_call" | custom-call | tf_op jit(solution)/shard_map/interior/pallas_call | solution.py:575
  19.7 0.0 collective-permute-done.4.refs_1_
  19.7 1.4 %update.1 = (f32[3,64,128]{2,1,0:T(8,128)}, f32[3,8,128]{2,1,0:T(8,128)}) custom-call(f32[7,64,128]{2,1,0:T(8,128)S(1)} %get-tuple-element.15.state_ref, s32[64,128]{1,0:T(8,128)S(1)} %get-tuple-element.16.cell_ref, f32[1040,128]{1,0:T(8,128)S(1)} %interior.1.acc_ref, f32[12,8,128]{2,1,0:T(8,128)S(1)} %get-tuple-element.17.refs_0_.parts_ref, ...), custom_call_target="tpu_custom_call" | custom-call | tf_op jit(solution)/shard_map/update/pallas_call | solution.py:595
Async XLA Ops:
  3.6 5.2 %collective-permute-start = (f32[12,8,128]{2,1,0:T(8,128)S(1)}, f32[12,8,128]{2,1,0:T(8,128)S(1)}, u32[]{:S(2)}, u32[]{:S(2)}) collective-permute-start(f32[12,8,128]{2,1,0:T(8,128)S(1)} %get-tuple-element.17.refs_0_.parts_ref), channel_id=1, source_target_pairs={{0,1},{1,0},{2,3},{3,2},{4,5},{5,4},{6,7},{7,6},{8,9},{9,8},{10,11... | collective-permute-start | bytes 147464 | tf_op jit(solution)/shard_map/ppermute | solution.py:537
  6.7 6.0 %collective-permute-start.1 = (f32[8,16,128]{2,1,0:T(8,128)S(1)}, f32[8,16,128]{2,1,0:T(8,128)S(1)}, u32[]{:S(2)}, u32[]{:S(2)}) collective-permute-start(f32[8,16,128]{2,1,0:T(8,128)S(1)} %get-tuple-element.22), channel_id=1, source_target_pairs={{0,8},{8,0},{16,24},{24,16},{1,9},{9,1},{17,25},{25,17},{2,10},{10... | collective-permute-start | bytes 196616 | tf_op jit(solution)/shard_map/ppermute | solution.py:481
  8.2 4.6 %collective-permute-start.2 = (f32[8,16,128]{2,1,0:T(8,128)S(1)}, f32[8,16,128]{2,1,0:T(8,128)S(1)}, u32[]{:S(2)}, u32[]{:S(2)}) collective-permute-start(f32[8,16,128]{2,1,0:T(8,128)S(1)} %get-tuple-element.23), channel_id=1, source_target_pairs={{0,4},{4,0},{8,16},{12,20},{16,8},{20,12},{24,28},{28,24},{1,5},{5... | collective-permute-start | bytes 196616 | tf_op jit(solution)/shard_map/ppermute | solution.py:489
  8.2 4.6 %collective-permute-start.3 = (f32[8,16,128]{2,1,0:T(8,128)S(1)}, f32[8,16,128]{2,1,0:T(8,128)S(1)}, u32[]{:S(2)}, u32[]{:S(2)}) collective-permute-start(f32[8,16,128]{2,1,0:T(8,128)S(1)} %get-tuple-element.24), channel_id=1, source_target_pairs={{0,4},{4,0},{1,5},{5,1},{2,6},{6,2},{3,7},{7,3},{8,12},{12,8},{9,1... | collective-permute-start | bytes 196616 | tf_op jit(solution)/shard_map/ppermute | solution.py:545
  11.6 8.1 %collective-permute-start.4 = (f32[8,8,128]{2,1,0:T(8,128)S(1)}, f32[8,8,128]{2,1,0:T(8,128)S(1)}, u32[]{:S(2)}, u32[]{:S(2)}) collective-permute-start(f32[8,8,128]{2,1,0:T(8,128)S(1)} %get-tuple-element.25), channel_id=1, source_target_pairs={{0,2},{1,3},{2,0},{3,1},{4,6},{5,7},{6,4},{7,5},{8,10},{9,11},{10,... | collective-permute-start | bytes 98312 | tf_op jit(solution)/shard_map/ppermute | solution.py:573

commit v3 on v2

--- a/solution.py
+++ b/solution.py
@@ -372,7 +372,8 @@
 
 
 def solved(total):
-    return [total[c] / total[3] for c in range(3)]
+    inverse = 1.0 / total[3]
+    return [total[c] * inverse for c in range(3)]
 
 
 def added(*terms):
@@ -450,16 +451,15 @@
                 taken = jnp.take_along_axis(line, low, axis=1, mode="promise_in_bounds")
                 at_cell[c] = jnp.where(chosen, taken, at_cell[c])
         r = state_ref[6, rows, :]
-        ratio = r / radius_ref
-        masses = ratio * ratio * ratio
-        rate = drag_coef * r * r
-        coupling = time_step * rate / masses
+        lag = time_step * drag_coef * radius_ref**3
+        push = time_step * radius_ref**3 / (r * r * r)
+        share = 1.0 / (r + lag)
         for c in range(3):
             velocity = state_ref[3 + c, rows, :]
             lever = velocity - spring * centred(state_ref[c, rows, :])
             force = -damping * (lever * weight - (sums(c) + sums(3 + c) + sums(6 + c)))
-            moved = velocity + time_step * force / masses
-            new_ref[c, rows, :] = (moved + coupling * at_cell[c]) / (1.0 + coupling)
+            moved = velocity + push * force
+            new_ref[c, rows, :] = (r * moved + lag * at_cell[c]) * share
         return carry
 
     lax.fori_loop(0, NT // 8, update_group, 0, unroll=8)

time: 21.4 us -> 21.1 us (0.986); the launches traced: 21.1 us -> 21.1 us
  starting transfers between devices: 6.23 us -> 6.77 us
  Pallas kernels: 14.1 us -> 13.6 us
    pallas_call x1, Pallas kernels: 2.82 us -> 2.28 us  [body(): pl.pallas_call(functools.partial(feature_kernel, paired), out_shape=(jax....]
    ppermute x1, starting transfers between devices: 1.14 us -> 1.68 us  [body(): slabs += (lax.ppermute(across[0], 'gz', [(i, i ^ 2) for i in range(4)]),)]
  transfers between devices with their start and end apart: 5 -> 5, of which waited for: 1 -> 1; matrix products, arithmetic and copies ran while one was open for 0% -> 0% of each run, Pallas kernels for 46% -> 44%
where the time goes in v3:
time: 21.1 us
  Pallas kernels  13.6 us (64%)
  starting transfers between devices  6.77 us (32%)
  between operations  0.67 us (3%)
    pallas_call x1, Pallas kernels, body(): pl.pallas_call(interior_kernel, out_shape=shape((NT + 1) * VROW, TILE), i...  6.98 us
    ppermute x1, starting transfers between devices, body(): beside = lax.ppermute(parts, 'gz', [(i, i ^ 1) for i in range(4)])  3.09 us
    pallas_call x1, Pallas kernels, body(): pl.pallas_call(deposit_kernel, out_shape=(shape(12, slab, LANES), face, f...  2.96 us
    pallas_call x1, Pallas kernels, body(): pl.pallas_call(functools.partial(feature_kernel, paired), out_shape=(jax....  2.28 us
    ppermute x1, starting transfers between devices, body(): slabs += (lax.ppermute(across[0], 'gz', [(i, i ^ 2) for i in range(4)]),)  1.68 us
    ppermute x1, starting transfers between devices, swapped(): first = lax.ppermute(first, axis, [(i, i ^ 1) for i in range(count)])  1.49 us
    pallas_call x1, Pallas kernels, body(): pl.pallas_call(functools.partial(update_kernel, paired), out_shape=(shape...  1.38 us
    ppermute x1, starting transfers between devices, body(): ya = yb = lax.ppermute(ya, 'gy', [(0, 1), (1, 0)])  0.51 us
  transfers between devices with their start and end apart: 5, of which 1 were waited for; matrix products, arithmetic and copies ran while one was open for 0% of the time, Pallas kernels for 44%

profile of v3, /device:TPU:0, one launch (start us, length us, event | category | flops | bytes accessed | tf_op | source)
XLA Modules:
  0.0 21.1 jit_solution(17539189945074799785)
XLA Ops:
  0.6 3.0 %deposit.1 = (f32[12,8,128]{2,1,0:T(8,128)S(1)}, f32[8,16,128]{2,1,0:T(8,128)S(1)}, f32[8,16,128]{2,1,0:T(8,128)S(1)}, f32[8,16,128]{2,1,0:T(8,128)S(1)}, f32[8,...) custom-call(f32[7,64,128]{2,1,0:T(8,128)} %bitcast.11, s32[64,128]{1,0:T(8,128)} %bitcast.12, ...), custom_call_target="tpu_custom_call" | custom-call | tf_op jit(solution)/shard_map/deposit/pallas_call | solution.py:515
  3.6 3.1 %collective-permute-start = (f32[12,8,128]{2,1,0:T(8,128)S(1)}, f32[12,8,128]{2,1,0:T(8,128)S(1)}, u32[]{:S(2)}, u32[]{:S(2)}) collective-permute-start(f32[12,8,128]{2,1,0:T(8,128)S(1)} %get-tuple-element.17.refs_0_.parts_ref), channel_id=1, source_target_pairs={{0,1},{1,0},{2,3},{3,2},{4,5},{5,4},{6,7},{7,6},{8,9},{9,8},{10,11... | collective-permute-start | bytes 147464 | tf_op jit(solution)/shard_map/ppermute | solution.py:537
  6.7 1.5 %collective-permute-start.1 = (f32[8,16,128]{2,1,0:T(8,128)S(1)}, f32[8,16,128]{2,1,0:T(8,128)S(1)}, u32[]{:S(2)}, u32[]{:S(2)}) collective-permute-start(f32[8,16,128]{2,1,0:T(8,128)S(1)} %get-tuple-element.22), channel_id=1, source_target_pairs={{0,8},{8,0},{16,24},{24,16},{1,9},{9,1},{17,25},{25,17},{2,10},{10... | collective-permute-start | bytes 196616 | tf_op jit(solution)/shard_map/ppermute | solution.py:481
  8.2 0.0 collective-permute-start.2
  8.2 0.5 %collective-permute-start.3 = (f32[8,16,128]{2,1,0:T(8,128)S(1)}, f32[8,16,128]{2,1,0:T(8,128)S(1)}, u32[]{:S(2)}, u32[]{:S(2)}) collective-permute-start(f32[8,16,128]{2,1,0:T(8,128)S(1)} %get-tuple-element.24), channel_id=1, source_target_pairs={{0,4},{4,0},{1,5},{5,1},{2,6},{6,2},{3,7},{7,3},{8,12},{12,8},{9,1... | collective-permute-start | bytes 196616 | tf_op jit(solution)/shard_map/ppermute | solution.py:545
  8.7 0.1 collective-permute-done.refs_1_.refs_0_
  8.8 2.3 %feature.1 = (bf16[8320,128]{1,0:T(8,128)(2,1)S(1)}, bf16[2176,128]{1,0:T(8,128)(2,1)S(1)}, bf16[1088,128]{1,0:T(8,128)(2,1)S(1)}, f32[1040,128]{1,0:T(8,128)S(1)}, f32[8,8,128]{2,1,0:T(8,128)S(1)}) custom-call(s32[8,64]{1,0:T(8,128)} %bitcast.13, s32[64]{0:T(128)} %bitcast.19, f32[7,64,128]{2,1,0:T(8,128)S(1)} %get-tuple-element.15.state_ref, ...), custom_call_target="tpu_custom_call" | custom-call | tf_op jit(solution)/shard_map/feature/pallas_call | solution.py:550
  11.1 1.7 %collective-permute-start.4 = (f32[8,8,128]{2,1,0:T(8,128)S(1)}, f32[8,8,128]{2,1,0:T(8,128)S(1)}, u32[]{:S(2)}, u32[]{:S(2)}) collective-permute-start(f32[8,8,128]{2,1,0:T(8,128)S(1)} %get-tuple-element.25), channel_id=1, source_target_pairs={{0,2},{1,3},{2,0},{3,1},{4,6},{5,7},{6,4},{7,5},{8,10},{9,11},{10,... | collective-permute-start | bytes 98312 | tf_op jit(solution)/shard_map/ppermute | solution.py:573
  12.7 0.0 collective-permute-done.1.xa_ref
  12.7 0.0 collective-permute-done.2.xb_ref
  12.7 0.0 collective-permute-done.3.ya_ref.yb_ref
  12.7 7.0 %interior.1.acc_ref = f32[1040,128]{1,0:T(8,128)S(1)} custom-call(s32[8,64]{1,0:T(8,128)} %bitcast.14, s32[64]{0:T(128)} %bitcast.20, s32[4]{0:T(128)} %bitcast.18, bf16[8320,128]{1,0:T(8,128)(2,1)S(1)} %get-tuple-element.18.near_ref, bf16[2176,128]{1,0:T(8,128)(2,1)S(1)} %get-tuple-element.19.own_turned_ref, ...), custom_call_target="tpu_custom_call" | custom-call | tf_op jit(solution)/shard_map/interior/pallas_call | solution.py:575
  19.7 0.0 collective-permute-done.4.refs_1_
  19.7 1.4 %update.1 = (f32[3,64,128]{2,1,0:T(8,128)}, f32[3,8,128]{2,1,0:T(8,128)}) custom-call(f32[7,64,128]{2,1,0:T(8,128)S(1)} %get-tuple-element.15.state_ref, s32[64,128]{1,0:T(8,128)S(1)} %get-tuple-element.16.cell_ref, f32[1040,128]{1,0:T(8,128)S(1)} %interior.1.acc_ref, f32[12,8,128]{2,1,0:T(8,128)S(1)} %get-tuple-element.17.refs_0_.parts_ref, ...), custom_call_target="tpu_custom_call" | custom-call | tf_op jit(solution)/shard_map/update/pallas_call | solution.py:595
Async XLA Ops:
  3.6 5.2 %collective-permute-start = (f32[12,8,128]{2,1,0:T(8,128)S(1)}, f32[12,8,128]{2,1,0:T(8,128)S(1)}, u32[]{:S(2)}, u32[]{:S(2)}) collective-permute-start(f32[12,8,128]{2,1,0:T(8,128)S(1)} %get-tuple-element.17.refs_0_.parts_ref), channel_id=1, source_target_pairs={{0,1},{1,0},{2,3},{3,2},{4,5},{5,4},{6,7},{7,6},{8,9},{9,8},{10,11... | collective-permute-start | bytes 147464 | tf_op jit(solution)/shard_map/ppermute | solution.py:537
  6.7 6.0 %collective-permute-start.1 = (f32[8,16,128]{2,1,0:T(8,128)S(1)}, f32[8,16,128]{2,1,0:T(8,128)S(1)}, u32[]{:S(2)}, u32[]{:S(2)}) collective-permute-start(f32[8,16,128]{2,1,0:T(8,128)S(1)} %get-tuple-element.22), channel_id=1, source_target_pairs={{0,8},{8,0},{16,24},{24,16},{1,9},{9,1},{17,25},{25,17},{2,10},{10... | collective-permute-start | bytes 196616 | tf_op jit(solution)/shard_map/ppermute | solution.py:481
  8.2 4.6 %collective-permute-start.2 = (f32[8,16,128]{2,1,0:T(8,128)S(1)}, f32[8,16,128]{2,1,0:T(8,128)S(1)}, u32[]{:S(2)}, u32[]{:S(2)}) collective-permute-start(f32[8,16,128]{2,1,0:T(8,128)S(1)} %get-tuple-element.23), channel_id=1, source_target_pairs={{0,4},{4,0},{8,16},{12,20},{16,8},{20,12},{24,28},{28,24},{1,5},{5... | collective-permute-start | bytes 196616 | tf_op jit(solution)/shard_map/ppermute | solution.py:489
  8.2 4.6 %collective-permute-start.3 = (f32[8,16,128]{2,1,0:T(8,128)S(1)}, f32[8,16,128]{2,1,0:T(8,128)S(1)}, u32[]{:S(2)}, u32[]{:S(2)}) collective-permute-start(f32[8,16,128]{2,1,0:T(8,128)S(1)} %get-tuple-element.24), channel_id=1, source_target_pairs={{0,4},{4,0},{1,5},{5,1},{2,6},{6,2},{3,7},{7,3},{8,12},{12,8},{9,1... | collective-permute-start | bytes 196616 | tf_op jit(solution)/shard_map/ppermute | solution.py:545
  11.1 8.7 %collective-permute-start.4 = (f32[8,8,128]{2,1,0:T(8,128)S(1)}, f32[8,8,128]{2,1,0:T(8,128)S(1)}, u32[]{:S(2)}, u32[]{:S(2)}) collective-permute-start(f32[8,8,128]{2,1,0:T(8,128)S(1)} %get-tuple-element.25), channel_id=1, source_target_pairs={{0,2},{1,3},{2,0},{3,1},{4,6},{5,7},{6,4},{7,5},{8,10},{9,11},{10,... | collective-permute-start | bytes 98312 | tf_op jit(solution)/shard_map/ppermute | solution.py:573
